TPU v7x, 32 devices: a whole 2x2x4 slice. The times are simulated.
32 devices in a mesh: front: 4 (over z), row: 8 (over y, x, core).
Axes of the slice: x: 2, y: 2, z: 4, core: 2. Of those that a mesh axis runs over, the one named last changes fastest.
Arguments:
- panels: bfloat16 [4, 1024, 1280], P('front', 'row'), may hold values from -6 to 6
- reflectors: bfloat16 [4, 1024, 512], P('front', 'row'), may hold values from -6 to 6
- block_coeffs: bfloat16 [4, 512, 512], P('front')
- block_mask: int32 [4, 8, 4], P('front', 'row'), may hold values 0 or 1
- block_starts: int32 [4, 4], P('front'), may hold values from 0 to 512, as said below
- carry_map: int32 [4, 256], P('front'), may hold values from 0 to 1023, as said below
Outputs:
- panels_out: bfloat16 [4, 1024, 1280], P('front', 'row')
Inputs may be any that keep to these rules, and one draw needn't show every extreme that they name: `block_starts`: nondecreasing along the reflector blocks of a front. `carry_map`: within a front the targets are distinct, and carried row i lands in the 128-row block number i % 8, which receives exactly 32 carried rows, its last row among them.
All inputs are finite; a program needn't handle non-finite values. No bound on the sum of `block_mask` on one device may be relied on, other than what follows from the above.
Results may differ from a plain program's by a relative error of at most 0.017.
Values may be sent and summed in bfloat16 or wider, within the bound.
A program may use at most 64 MiB of HBM per device.

v0:
```python
import jax
import jax.numpy as jnp
from jax import lax
from jax.sharding import PartitionSpec as P

PW = 256
NPANEL = 5


def from_behind(value, axis, steps):
    count = lax.axis_size(axis)
    initial, last = (max(0, -steps), min(count, count - steps))
    return lax.ppermute(value, axis, [(source, source + steps) for source in range(initial, last)])


def spread_rows(pieces):
    return lax.all_to_all(pieces, "row", split_axis=1, concat_axis=1, tiled=True)


def pass_along(pieces):
    return from_behind(pieces, "front", 1)


def local(panels, reflectors, block_coeffs, block_mask, block_starts, carry_map):
    row_count = lax.axis_size("row")
    front_count = lax.axis_size("front")
    row_index = lax.axis_index("row")
    front_index = lax.axis_index("front")
    row_span = panels.shape[1]
    tail_start = 3 * row_count // 4
    quarter = row_count - tail_start
    per_source = row_span // row_count
    global_rows = row_index * row_span + jnp.arange(row_span, dtype=jnp.int32)
    mask_full = jnp.repeat(jnp.repeat(block_mask[0], 128, axis=0), 128, axis=1)
    start_cols = jnp.repeat(block_starts[0], 128)
    retained = (mask_full == 1) & (global_rows[:, None] >= start_cols[None, :])
    effective = jnp.where(retained, reflectors[0], jnp.zeros_like(reflectors[0]))
    coeffs = block_coeffs[0]
    target_table = carry_map[0].reshape(quarter, per_source, row_count)
    own_targets = lax.dynamic_slice_in_dim(target_table, row_index, 1, 2)[:, :, 0]
    local_target = (own_targets.T - row_index * row_span).reshape(-1)
    placement = (jnp.arange(row_span, dtype=jnp.int32)[:, None] == local_target[None, :]).astype(
        jnp.bfloat16
    )
    is_tail = row_index >= tail_start
    initial = jnp.zeros((per_source, quarter, PW), jnp.bfloat16)

    def advance(step_index, state):
        out_buffer, incoming = state
        panel_index = step_index - front_index
        is_live = (panel_index >= 0) & (panel_index < NPANEL)
        panel_pos = jnp.clip(panel_index, 0, NPANEL - 1) * PW
        moved = jnp.dot(
            placement, incoming.reshape(row_span // 4, PW), preferred_element_type=jnp.float32
        )
        own_panel = lax.dynamic_slice_in_dim(panels[0], panel_pos, PW, 1)
        assembled = (own_panel.astype(jnp.float32) + moved).astype(jnp.bfloat16)
        partial_value = lax.dot_general(
            effective, assembled, (((0,), (0,)), ((), ())), preferred_element_type=jnp.float32
        )
        totals = lax.psum(partial_value, "row")
        mixed = lax.dot_general(
            coeffs,
            totals.astype(jnp.bfloat16),
            (((0,), (0,)), ((), ())),
            preferred_element_type=jnp.float32,
        ).astype(jnp.bfloat16)
        result = (
            assembled.astype(jnp.float32)
            - jnp.dot(effective, mixed, preferred_element_type=jnp.float32)
        ).astype(jnp.bfloat16)
        current = lax.dynamic_slice_in_dim(out_buffer, panel_pos, PW, 1)
        out_buffer = lax.dynamic_update_slice_in_dim(
            out_buffer, jnp.where(is_live, result, current), panel_pos, 1
        )
        outgoing = jnp.where(is_tail, result, jnp.zeros_like(result)).reshape(
            per_source, row_count, PW
        )
        following = pass_along(spread_rows(outgoing)[:, tail_start:, :])
        return (out_buffer, following)

    out_buffer, leftover = lax.fori_loop(
        0, front_count + NPANEL - 1, advance, (jnp.zeros_like(panels[0]), initial)
    )
    return out_buffer[None]


def solution(mesh):
    in_specs = (
        P("front", "row", None),
        P("front", "row", None),
        P("front", None, None),
        P("front", "row", None),
        P("front", None),
        P("front", None),
    )
    out_specs = P("front", "row", None)
    return jax.shard_map(local, mesh=mesh, in_specs=in_specs, out_specs=out_specs, check_vma=False)
```

profile of v0, /device:TPU:25, one launch (start us, length us, event | category | flops | bytes accessed | tf_op | source)
XLA Modules:
  0.0 361.2 jit_solution(2206078311789844931)
XLA Ops:
  0.0 0.7 copy-done
  0.7 0.7 copy-done.4
  1.4 0.5 broadcast.34
  2.1 0.7 reduce.5
  3.3 1.0 and_select_fusion
  4.4 356.1 %while.16 = (s32[]{:T(128)}, bf16[128,1280]{1,0:T(8,128)(2,1)S(1)}, bf16[16,2,256]{2,0,1:T(8,128)(2,1)S(1)}, s32[]{:T(128)}, bf16[1,128,1280]{2,1,0:T(8,128)(2,1...) while((s32[]{:T(128)}, bf16[128,1280]{1,0:T(8,128)(2,1)S(1)}, ...), condition=%wide.region_2.3_spmd.clone, body=%wide.region_0.2_spmd.clone.sunk | while | flops 203956240 | bytes 3260838 | solution.py:82
  4.4 1.0 fusion.33
  5.7 27.6 %all-reduce.1 = bf16[512,256]{0,1:T(8,128)(2,1)S(1)} all-reduce(f32[512,256]{0,1:T(8,128)S(1)} %convolution_bitcast_fusion.2), channel_id=1, replica_groups=mesh['front'=4,'row'=8] {'row'}, use_global_device_ids=true, to_apply=%region_1.1 | all-reduce | flops 131072 | bytes 786432 | tf_op jit(solution)/shard_map/while/body/eval_jaxpr/psum | solution.py:61
  33.8 10.1 %all_to_all.11 = bf16[16,8,256]{2,0,1:T(8,128)(2,1)S(1)} all-to-all(bf16[16,8,256]{2,0,1:T(8,128)(2,1)S(1)} %copy.19), channel_id=1, replica_groups=mesh['front'=4,'row'=8] {'row'}, dimensions={1} | all-to-all | bytes 131072 | tf_op jit(solution)/shard_map/while/body/eval_jaxpr/all_to_all | solution.py:17
  43.9 1.3 collective-permute-start
  45.2 3.2 collective-permute-done
  48.4 1.0 fusion.33
  49.6 28.3 %all-reduce.1 = bf16[512,256]{0,1:T(8,128)(2,1)S(1)} all-reduce(f32[512,256]{0,1:T(8,128)S(1)} %convolution_bitcast_fusion.2), channel_id=1, replica_groups=mesh['front'=4,'row'=8] {'row'}, use_global_device_ids=true, to_apply=%region_1.1 | all-reduce | flops 131072 | bytes 786432 | tf_op jit(solution)/shard_map/while/body/eval_jaxpr/psum | solution.py:61
  78.4 10.1 %all_to_all.11 = bf16[16,8,256]{2,0,1:T(8,128)(2,1)S(1)} all-to-all(bf16[16,8,256]{2,0,1:T(8,128)(2,1)S(1)} %copy.19), channel_id=1, replica_groups=mesh['front'=4,'row'=8] {'row'}, dimensions={1} | all-to-all | bytes 131072 | tf_op jit(solution)/shard_map/while/body/eval_jaxpr/all_to_all | solution.py:17
  88.5 1.3 collective-permute-start
  89.8 3.2 collective-permute-done
  93.0 1.0 fusion.33
  94.2 28.3 %all-reduce.1 = bf16[512,256]{0,1:T(8,128)(2,1)S(1)} all-reduce(f32[512,256]{0,1:T(8,128)S(1)} %convolution_bitcast_fusion.2), channel_id=1, replica_groups=mesh['front'=4,'row'=8] {'row'}, use_global_device_ids=true, to_apply=%region_1.1 | all-reduce | flops 131072 | bytes 786432 | tf_op jit(solution)/shard_map/while/body/eval_jaxpr/psum | solution.py:61
  123.0 10.1 %all_to_all.11 = bf16[16,8,256]{2,0,1:T(8,128)(2,1)S(1)} all-to-all(bf16[16,8,256]{2,0,1:T(8,128)(2,1)S(1)} %copy.19), channel_id=1, replica_groups=mesh['front'=4,'row'=8] {'row'}, dimensions={1} | all-to-all | bytes 131072 | tf_op jit(solution)/shard_map/while/body/eval_jaxpr/all_to_all | solution.py:17
  133.0 1.3 collective-permute-start
  134.3 3.2 collective-permute-done
  137.6 1.0 fusion.33
  138.8 28.3 %all-reduce.1 = bf16[512,256]{0,1:T(8,128)(2,1)S(1)} all-reduce(f32[512,256]{0,1:T(8,128)S(1)} %convolution_bitcast_fusion.2), channel_id=1, replica_groups=mesh['front'=4,'row'=8] {'row'}, use_global_device_ids=true, to_apply=%region_1.1 | all-reduce | flops 131072 | bytes 786432 | tf_op jit(solution)/shard_map/while/body/eval_jaxpr/psum | solution.py:61
  167.6 10.1 %all_to_all.11 = bf16[16,8,256]{2,0,1:T(8,128)(2,1)S(1)} all-to-all(bf16[16,8,256]{2,0,1:T(8,128)(2,1)S(1)} %copy.19), channel_id=1, replica_groups=mesh['front'=4,'row'=8] {'row'}, dimensions={1} | all-to-all | bytes 131072 | tf_op jit(solution)/shard_map/while/body/eval_jaxpr/all_to_all | solution.py:17
  177.6 1.3 collective-permute-start
  178.9 3.2 collective-permute-done
  182.2 1.0 fusion.33
  183.4 28.3 %all-reduce.1 = bf16[512,256]{0,1:T(8,128)(2,1)S(1)} all-reduce(f32[512,256]{0,1:T(8,128)S(1)} %convolution_bitcast_fusion.2), channel_id=1, replica_groups=mesh['front'=4,'row'=8] {'row'}, use_global_device_ids=true, to_apply=%region_1.1 | all-reduce | flops 131072 | bytes 786432 | tf_op jit(solution)/shard_map/while/body/eval_jaxpr/psum | solution.py:61
  212.2 10.1 %all_to_all.11 = bf16[16,8,256]{2,0,1:T(8,128)(2,1)S(1)} all-to-all(bf16[16,8,256]{2,0,1:T(8,128)(2,1)S(1)} %copy.19), channel_id=1, replica_groups=mesh['front'=4,'row'=8] {'row'}, dimensions={1} | all-to-all | bytes 131072 | tf_op jit(solution)/shard_map/while/body/eval_jaxpr/all_to_all | solution.py:17
  222.2 1.3 collective-permute-start
  223.5 3.2 collective-permute-done
  226.7 1.0 fusion.33
  228.0 28.3 %all-reduce.1 = bf16[512,256]{0,1:T(8,128)(2,1)S(1)} all-reduce(f32[512,256]{0,1:T(8,128)S(1)} %convolution_bitcast_fusion.2), channel_id=1, replica_groups=mesh['front'=4,'row'=8] {'row'}, use_global_device_ids=true, to_apply=%region_1.1 | all-reduce | flops 131072 | bytes 786432 | tf_op jit(solution)/shard_map/while/body/eval_jaxpr/psum | solution.py:61
  256.3 0.5 select_bitcast_fusion.2
  256.8 10.1 %all_to_all.11 = bf16[16,8,256]{2,0,1:T(8,128)(2,1)S(1)} all-to-all(bf16[16,8,256]{2,0,1:T(8,128)(2,1)S(1)} %copy.19), channel_id=1, replica_groups=mesh['front'=4,'row'=8] {'row'}, dimensions={1} | all-to-all | bytes 131072 | tf_op jit(solution)/shard_map/while/body/eval_jaxpr/all_to_all | solution.py:17
  266.8 1.3 collective-permute-start
  268.1 3.2 collective-permute-done
  271.3 1.0 fusion.33
  272.6 28.3 %all-reduce.1 = bf16[512,256]{0,1:T(8,128)(2,1)S(1)} all-reduce(f32[512,256]{0,1:T(8,128)S(1)} %convolution_bitcast_fusion.2), channel_id=1, replica_groups=mesh['front'=4,'row'=8] {'row'}, use_global_device_ids=true, to_apply=%region_1.1 | all-reduce | flops 131072 | bytes 786432 | tf_op jit(solution)/shard_map/while/body/eval_jaxpr/psum | solution.py:61
  301.3 10.1 %all_to_all.11 = bf16[16,8,256]{2,0,1:T(8,128)(2,1)S(1)} all-to-all(bf16[16,8,256]{2,0,1:T(8,128)(2,1)S(1)} %copy.19), channel_id=1, replica_groups=mesh['front'=4,'row'=8] {'row'}, dimensions={1} | all-to-all | bytes 131072 | tf_op jit(solution)/shard_map/while/body/eval_jaxpr/all_to_all | solution.py:17
  311.4 1.3 collective-permute-start
  312.7 3.2 collective-permute-done
  315.9 1.0 fusion.33
  317.2 28.3 %all-reduce.1 = bf16[512,256]{0,1:T(8,128)(2,1)S(1)} all-reduce(f32[512,256]{0,1:T(8,128)S(1)} %convolution_bitcast_fusion.2), channel_id=1, replica_groups=mesh['front'=4,'row'=8] {'row'}, use_global_device_ids=true, to_apply=%region_1.1 | all-reduce | flops 131072 | bytes 786432 | tf_op jit(solution)/shard_map/while/body/eval_jaxpr/psum | solution.py:61
  345.9 10.1 %all_to_all.11 = bf16[16,8,256]{2,0,1:T(8,128)(2,1)S(1)} all-to-all(bf16[16,8,256]{2,0,1:T(8,128)(2,1)S(1)} %copy.19), channel_id=1, replica_groups=mesh['front'=4,'row'=8] {'row'}, dimensions={1} | all-to-all | bytes 131072 | tf_op jit(solution)/shard_map/while/body/eval_jaxpr/all_to_all | solution.py:17
  356.0 1.3 collective-permute-start
  357.3 3.2 collective-permute-done
  360.5 0.7 copy-done.1
  (64 shorter events, 6.5 us)
Async XLA Ops:
  0.0 0.7 copy-start
  0.7 0.7 copy-start.4
  1.4 0.7 copy-start.2
  1.4 3.0 copy-start.3
  43.9 4.5 %collective-permute-start = (bf16[16,2,256]{2,0,1:T(8,128)(2,1)S(1)}, bf16[16,2,256]{2,0,1:T(8,128)(2,1)S(1)}, u32[]{:S(2)}, u32[]{:S(2)}) collective-permute-start(bf16[16,2,256]{2,0,1:T(8,128)(2,1)S(1)} %slice.10), channel_id=1, source_target_pairs={{0,8},{8,16},{16,24},{1,9},{9,17},{17,25},{2,10},{10,18},{18,26},{... | collective-permute-start | bytes 49160 | tf_op jit(solution)/shard_map/while/body/eval_jaxpr/ppermute | solution.py:13
  88.5 4.5 %collective-permute-start = (bf16[16,2,256]{2,0,1:T(8,128)(2,1)S(1)}, bf16[16,2,256]{2,0,1:T(8,128)(2,1)S(1)}, u32[]{:S(2)}, u32[]{:S(2)}) collective-permute-start(bf16[16,2,256]{2,0,1:T(8,128)(2,1)S(1)} %slice.10), channel_id=1, source_target_pairs={{0,8},{8,16},{16,24},{1,9},{9,17},{17,25},{2,10},{10,18},{18,26},{... | collective-permute-start | bytes 49160 | tf_op jit(solution)/shard_map/while/body/eval_jaxpr/ppermute | solution.py:13
  133.0 4.5 %collective-permute-start = (bf16[16,2,256]{2,0,1:T(8,128)(2,1)S(1)}, bf16[16,2,256]{2,0,1:T(8,128)(2,1)S(1)}, u32[]{:S(2)}, u32[]{:S(2)}) collective-permute-start(bf16[16,2,256]{2,0,1:T(8,128)(2,1)S(1)} %slice.10), channel_id=1, source_target_pairs={{0,8},{8,16},{16,24},{1,9},{9,17},{17,25},{2,10},{10,18},{18,26},{... | collective-permute-start | bytes 49160 | tf_op jit(solution)/shard_map/while/body/eval_jaxpr/ppermute | solution.py:13
  177.6 4.5 %collective-permute-start = (bf16[16,2,256]{2,0,1:T(8,128)(2,1)S(1)}, bf16[16,2,256]{2,0,1:T(8,128)(2,1)S(1)}, u32[]{:S(2)}, u32[]{:S(2)}) collective-permute-start(bf16[16,2,256]{2,0,1:T(8,128)(2,1)S(1)} %slice.10), channel_id=1, source_target_pairs={{0,8},{8,16},{16,24},{1,9},{9,17},{17,25},{2,10},{10,18},{18,26},{... | collective-permute-start | bytes 49160 | tf_op jit(solution)/shard_map/while/body/eval_jaxpr/ppermute | solution.py:13
  222.2 4.5 %collective-permute-start = (bf16[16,2,256]{2,0,1:T(8,128)(2,1)S(1)}, bf16[16,2,256]{2,0,1:T(8,128)(2,1)S(1)}, u32[]{:S(2)}, u32[]{:S(2)}) collective-permute-start(bf16[16,2,256]{2,0,1:T(8,128)(2,1)S(1)} %slice.10), channel_id=1, source_target_pairs={{0,8},{8,16},{16,24},{1,9},{9,17},{17,25},{2,10},{10,18},{18,26},{... | collective-permute-start | bytes 49160 | tf_op jit(solution)/shard_map/while/body/eval_jaxpr/ppermute | solution.py:13
  266.8 4.5 %collective-permute-start = (bf16[16,2,256]{2,0,1:T(8,128)(2,1)S(1)}, bf16[16,2,256]{2,0,1:T(8,128)(2,1)S(1)}, u32[]{:S(2)}, u32[]{:S(2)}) collective-permute-start(bf16[16,2,256]{2,0,1:T(8,128)(2,1)S(1)} %slice.10), channel_id=1, source_target_pairs={{0,8},{8,16},{16,24},{1,9},{9,17},{17,25},{2,10},{10,18},{18,26},{... | collective-permute-start | bytes 49160 | tf_op jit(solution)/shard_map/while/body/eval_jaxpr/ppermute | solution.py:13
  311.4 4.5 %collective-permute-start = (bf16[16,2,256]{2,0,1:T(8,128)(2,1)S(1)}, bf16[16,2,256]{2,0,1:T(8,128)(2,1)S(1)}, u32[]{:S(2)}, u32[]{:S(2)}) collective-permute-start(bf16[16,2,256]{2,0,1:T(8,128)(2,1)S(1)} %slice.10), channel_id=1, source_target_pairs={{0,8},{8,16},{16,24},{1,9},{9,17},{17,25},{2,10},{10,18},{18,26},{... | collective-permute-start | bytes 49160 | tf_op jit(solution)/shard_map/while/body/eval_jaxpr/ppermute | solution.py:13
  356.0 4.5 %collective-permute-start = (bf16[16,2,256]{2,0,1:T(8,128)(2,1)S(1)}, bf16[16,2,256]{2,0,1:T(8,128)(2,1)S(1)}, u32[]{:S(2)}, u32[]{:S(2)}) collective-permute-start(bf16[16,2,256]{2,0,1:T(8,128)(2,1)S(1)} %slice.10), channel_id=1, source_target_pairs={{0,8},{8,16},{16,24},{1,9},{9,17},{17,25},{2,10},{10,18},{18,26},{... | collective-permute-start | bytes 49160 | tf_op jit(solution)/shard_map/while/body/eval_jaxpr/ppermute | solution.py:13
  360.5 0.7 copy-start.1
where the time goes:
time: 364 us; the launch traced here: 361 us
  blocking collectives  306 us (84%)
  waiting for transfers between devices  25.4 us (7%)
  matrix products  13.6 us (4%)
  starting transfers between devices  10.2 us (3%)
    psum x8, blocking collectives, advance(): totals = lax.psum(partial_value, 'row')  225 us
    all_to_all x8, blocking collectives, spread_rows(): lax.all_to_all(pieces, 'row', split_axis=1, concat_axis=1, tiled=True)  80.5 us
    ppermute x8, waiting for transfers between devices, from_behind(): lax.ppermute(value, axis, [(source, source + steps) for source in range(i...  25.4 us
    ppermute x8, starting transfers between devices, from_behind(): lax.ppermute(value, axis, [(source, source + steps) for source in range(i...  10.2 us
    dot_general x8, matrix products, advance(): jnp.dot(placement, incoming.reshape(row_span // 4, PW), preferred_element...  7.85 us
  transfers between devices with their start and end apart: 8, of which 8 were waited for; matrix products, arithmetic and copies ran while one was open for 0% of the time, Pallas kernels for 0%

commit v1 on v0

v1 whole, which is shorter than its diff:
```python
import functools

import jax
import jax.numpy as jnp
from jax import lax
from jax.experimental import pallas as pl
from jax.experimental.pallas import tpu as pltpu
from jax.sharding import PartitionSpec as P

F32 = jnp.float32
BF16 = jnp.bfloat16
LANES = 128


def dot(a, b):
    return jnp.dot(a, b, preferred_element_type=F32)


def dot_nt(a, b):
    return lax.dot_general(a, b, (((1,), (1,)), ((), ())), preferred_element_type=F32)


def kernel(
    n, fronts, width,
    mask_ref, starts_ref, panels_ref, refl_ref, coeffs_ref, cmap_ref, out_ref,
    pt, pr, ea, place, ec, cin, sacc, rt, rr,
    e_send, e_recv, s_send, s_recv, p_send, p_recv, r_send, r_recv, z_send, z_recv,
):
    me = lax.axis_index("row")
    front = lax.axis_index("front")
    span = panels_ref.shape[1]
    cols = panels_ref.shape[2]
    rows = n * span
    tail = 3 * rows // 4
    chips = n // 2
    chip = me // 2
    core = me % 2
    sibling = chip * 2 + (1 - core)

    def at_row(r):
        return {"front": front, "row": r}

    def at_front(f):
        return {"front": f, "row": me}

    def remote(src, dst, ss, rs, dev):
        return pltpu.make_async_remote_copy(
            src_ref=src, dst_ref=dst, send_sem=ss, recv_sem=rs,
            device_id=dev, device_id_type=pl.DeviceIdType.MESH,
        )

    def blk(r):
        return pl.ds(pl.multiple_of(r * span, span), span)

    def strip(r):
        return pl.ds(pl.multiple_of(r * width, 16), width)

    barrier = pltpu.get_barrier_semaphore()
    for k in range(1, n):
        pl.semaphore_signal(barrier, inc=1, device_id=at_row((me + k) % n),
                            device_id_type=pl.DeviceIdType.MESH)

    @pl.when(front > 0)
    def _():
        pl.semaphore_signal(barrier, inc=1, device_id=at_front(front - 1),
                            device_id_type=pl.DeviceIdType.MESH)

    @pl.when(front < fronts - 1)
    def _():
        pl.semaphore_signal(barrier, inc=1, device_id=at_front(front + 1),
                            device_id_type=pl.DeviceIdType.MESH)

    row_ids = me * span + lax.broadcasted_iota(jnp.int32, (span, LANES), 0)
    for j in range(refl_ref.shape[2] // LANES):
        keep = jnp.logical_and(row_ids >= starts_ref[0, j], mask_ref[0, 0, j] == 1)
        block = refl_ref[0, :, j * LANES:(j + 1) * LANES]
        ea[blk(me), j * LANES:(j + 1) * LANES] = jnp.where(keep, block, jnp.zeros_like(block))

    pl.semaphore_wait(barrier, n - 1 + jnp.where(front > 0, 1, 0)
                      + jnp.where(front < fronts - 1, 1, 0))

    e_out = []
    for k in range(1, chips):
        c = remote(ea.at[blk(me)], ea.at[blk(me)], e_send.at[k], e_recv.at[k],
                   at_row(((chip + k) % chips) * 2 + core))
        c.start()
        e_out.append(c)
    c = remote(ea.at[blk(me)], ea.at[blk(me)], s_send.at[0], s_recv.at[0], at_row(sibling))
    c.start()
    e_out.append(c)

    for j in range(cols // LANES):
        pt[j * LANES:(j + 1) * LANES, :] = panels_ref[0, :, j * LANES:(j + 1) * LANES].T
    if pt.shape[0] > cols:
        pt[cols:, :] = jnp.zeros((pt.shape[0] - cols, span), BF16)
    p_out = []
    for k in range(1, n):
        peer = (me + k) % n
        c = remote(pt.at[strip(peer)], pr.at[:, blk(me)], p_send.at[k], p_recv.at[k], at_row(peer))
        c.start()
        p_out.append(c)
    pr[:, blk(me)] = pt[strip(me), :]

    ncar = cmap_ref.shape[1]
    targets = jnp.broadcast_to(cmap_ref[...], (LANES, ncar)).T
    lane = lax.broadcasted_iota(jnp.int32, (ncar, LANES), 1)
    for b in range(rows // LANES):
        place[:, b * LANES:(b + 1) * LANES] = jnp.where(
            targets == lane + b * LANES, 1.0, 0.0).astype(BF16)

    for k in range(1, chips):
        src = ((chip + chips - k) % chips) * 2 + core
        e_out[k - 1].wait_recv()
        c = remote(ea.at[blk(src)], ea.at[blk(src)], s_send.at[k], s_recv.at[k], at_row(sibling))
        c.start()
        e_out.append(c)
    for c in e_out[chips - 1:]:
        c.wait_recv()

    ec[...] = dot(place[...], ea[...]).astype(BF16)

    for c in p_out:
        c.wait_recv()
    sacc[...] = dot(pr[...], ea[...])

    z_copy = remote(rt.at[:, pl.ds(tail, rows - tail)], cin, z_send, z_recv,
                    at_front((front + 1) % fronts))

    @pl.when(front == 0)
    def _():
        cin[...] = jnp.zeros_like(cin)

    @pl.when(front > 0)
    def _():
        z_copy.wait_recv()

    carried = cin[...]
    wcoef = (sacc[...] + dot(carried, ec[...])).astype(BF16)
    mixed = dot(wcoef, coeffs_ref[0]).astype(BF16)

    def finish(lo, hi):
        assembled = (pr[:, lo:hi].astype(F32) + dot(carried, place[:, lo:hi])).astype(BF16)
        rt[:, lo:hi] = (assembled.astype(F32) - dot_nt(mixed, ea[lo:hi, :])).astype(BF16)

    finish(tail, rows)

    @pl.when(front < fronts - 1)
    def _():
        z_copy.start()

    finish(0, tail)

    r_out = []
    for k in range(1, n):
        peer = (me + k) % n
        c = remote(rt.at[:, blk(peer)], rr.at[strip(me)], r_send.at[k], r_recv.at[k], at_row(peer))
        c.start()
        r_out.append(c)
    rr[strip(me), :] = rt[:, blk(me)]
    for c in r_out:
        c.wait_recv()
    for j in range(cols // LANES):
        out_ref[0, :, j * LANES:(j + 1) * LANES] = rr[j * LANES:(j + 1) * LANES, :].T

    for c in e_out + p_out + r_out:
        c.wait_send()

    @pl.when(front < fronts - 1)
    def _():
        z_copy.wait_send()


def local(n, fronts, panels, reflectors, block_coeffs, block_mask, block_starts, carry_map):
    _, span, cols = panels.shape
    k = reflectors.shape[2]
    rows = n * span
    ncar = carry_map.shape[1]
    width = -(-cols // (16 * n)) * 16
    dma = pltpu.SemaphoreType.DMA
    vmem = pl.BlockSpec(memory_space=pltpu.VMEM)
    smem = pl.BlockSpec(memory_space=pltpu.SMEM)
    return pl.pallas_call(
        functools.partial(kernel, n, fronts, width),
        out_shape=jax.ShapeDtypeStruct(panels.shape, panels.dtype),
        in_specs=[smem, smem, vmem, vmem, vmem, vmem],
        out_specs=vmem,
        scratch_shapes=[
            pltpu.VMEM((n * width, span), BF16),
            pltpu.VMEM((width, rows), BF16),
            pltpu.VMEM((rows, k), BF16),
            pltpu.VMEM((ncar, rows), BF16),
            pltpu.VMEM((ncar, k), BF16),
            pltpu.VMEM((width, ncar), BF16),
            pltpu.VMEM((width, k), F32),
            pltpu.VMEM((width, rows), BF16),
            pltpu.VMEM((n * width, span), BF16),
            dma((n // 2,)), dma((n // 2,)), dma((n // 2,)), dma((n // 2,)),
            dma((n,)), dma((n,)), dma((n,)), dma((n,)), dma, dma,
        ],
        compiler_params=pltpu.CompilerParams(
            collective_id=0, has_side_effects=True, vmem_limit_bytes=48 * 1024 * 1024),
    )(block_mask, block_starts, panels, reflectors, block_coeffs, carry_map)


def solution(mesh):
    in_specs = (
        P("front", "row", None),
        P("front", "row", None),
        P("front", None, None),
        P("front", "row", None),
        P("front", None),
        P("front", None),
    )
    body = functools.partial(local, mesh.shape["row"], mesh.shape["front"])
    return jax.shard_map(body, mesh=mesh, in_specs=in_specs,
                         out_specs=P("front", "row", None), check_vma=False)
```

time: 364 us -> 36.9 us (0.10)
  blocking collectives: 306 us -> 0 us
  Pallas kernels: 0 us -> 31 us
  waiting for transfers between devices: 25.4 us -> 0 us
  matrix products: 13.6 us -> 0 us
  starting transfers between devices: 10.2 us -> 0 us
    psum x8 -> x0, blocking collectives: 225 us -> none  [advance(): totals = lax.psum(partial_value, 'row')]
    all_to_all x8 -> x0, blocking collectives: 80.5 us -> none  [spread_rows(): lax.all_to_all(pieces, 'row', split_axis=1, concat_axis=1, tiled=True)]
    pallas_call x0 -> x1, Pallas kernels: none -> 31 us  [local(): pl.pallas_call(functools.partial(kernel, n, fronts, width), out_shape=jax...]
    ppermute x8 -> x0, waiting for transfers between devices: 25.4 us -> none  [from_behind(): lax.ppermute(value, axis, [(source, source + steps) for source in range(i...]
    dot_general x24 -> x0, matrix products: 13.6 us -> none  [the longest x8 7.85 us: advance(): jnp.dot(placement, incoming.reshape(row_span // 4, PW), preferred_element...]
    ppermute x8 -> x0, starting transfers between devices: 10.2 us -> none  [from_behind(): lax.ppermute(value, axis, [(source, source + steps) for source in range(i...]
  transfers between devices with their start and end apart: 8 -> 0, of which waited for: 8 -> 0; matrix products, arithmetic and copies ran while one was open for 0% -> 0% of each run, Pallas kernels for 0% -> 0%
where the time goes in v1:
time: 36.9 us; the launch traced here: 36.7 us
  Pallas kernels  31 us (84%)
  local copies, waits for them, and re-layouts  5.63 us (15%)
    pallas_call x1, Pallas kernels, local(): pl.pallas_call(functools.partial(kernel, n, fronts, width), out_shape=jax...  31 us
    unnamed x13, local copies, waits for them, and re-layouts  5.63 us

profile of v1, /device:TPU:25, one launch (start us, length us, event | category | flops | bytes accessed | tf_op | source)
XLA Modules:
  0.0 36.7 jit_solution(12559776979711972138)
XLA Ops:
  0.0 0.0 copy-start
  0.0 1.0 %copy-done = bf16[1,512,512]{2,1,0:T(8,128)(2,1)S(1)} copy-done((bf16[1,512,512]{2,1,0:T(8,128)(2,1)S(1)}, bf16[1,512,512]{2,1,0:T(8,128)(2,1)}, u32[]{:S(2)}) %copy-start) | copy-done | bytes 524312
  1.0 0.0 copy-start.1
  1.0 1.0 %copy-done.1 = bf16[1,128,1280]{2,1,0:T(8,128)(2,1)S(1)} copy-done((bf16[1,128,1280]{2,1,0:T(8,128)(2,1)S(1)}, bf16[1,128,1280]{2,1,0:T(8,128)(2,1)}, u32[]{:S(2)}) %copy-start.1) | copy-done | bytes 327704
  2.0 0.0 copy-start.2
  2.0 0.9 %copy-done.2 = bf16[1,128,512]{2,1,0:T(8,128)(2,1)S(1)} copy-done((bf16[1,128,512]{2,1,0:T(8,128)(2,1)S(1)}, bf16[1,128,512]{2,1,0:T(8,128)(2,1)}, u32[]{:S(2)}) %copy-start.2) | copy-done | bytes 131096
  2.9 0.0 copy-start.3
  2.9 0.7 %copy-done.3 = s32[1,256]{1,0:T(1,128)S(1)} copy-done((s32[1,256]{1,0:T(1,128)S(1)}, s32[1,256]{1,0:T(1,128)}, u32[]{:S(2)}) %copy-start.3) | copy-done | bytes 1048
  3.6 0.0 copy-start.4
  3.6 0.7 %copy-done.4 = s32[1,1,4]{2,1,0:T(1,128)S(1)} copy-done((s32[1,1,4]{2,1,0:T(1,128)S(1)}, s32[1,1,4]{2,1,0:T(1,128)}, u32[]{:S(2)}) %copy-start.4) | copy-done | bytes 40
  4.3 0.0 copy-start.5
  4.3 0.7 %copy-done.5 = s32[1,4]{1,0:T(1,128)S(1)} copy-done((s32[1,4]{1,0:T(1,128)S(1)}, s32[1,4]{1,0:T(1,128)}, u32[]{:S(2)}) %copy-start.5) | copy-done | bytes 40
  4.9 31.0 %shard_map.64 = bf16[1,128,1280]{2,1,0:T(8,128)(2,1)S(1)} custom-call(s32[1,1,4]{2,1,0:T(1,128)S(1)} %copy-done.4, s32[1,4]{1,0:T(1,128)S(1)} %copy-done.5, bf16[1,128,1280]{2,1,0:T(8,128)(2,1)S(1)} %copy-done.1, bf16[1,128,512]{2,1,0:T(8,128)(2,1)S(1)} %copy-done.2, bf16[1,512,512]{2,1,0:T(8,128)(2,1)S(1)} %copy-done, s32[1,256]{1,0:T(1,128)S(1)} %copy-done.3), custom_call_target="tpu_custom_call" | custom-call | tf_op jit(solution)/shard_map/pallas_call | solution.py:182
  35.9 0.7 %copy.8 = bf16[1,128,1280]{2,1,0:T(8,128)(2,1)} copy(bf16[1,128,1280]{2,1,0:T(8,128)(2,1)S(1)} %shard_map.64) | data formatting | bytes 655360
Async XLA Ops:
  0.0 1.0 %copy-start = (bf16[1,512,512]{2,1,0:T(8,128)(2,1)S(1)}, bf16[1,512,512]{2,1,0:T(8,128)(2,1)}, u32[]{:S(2)}) copy-start(bf16[1,512,512]{2,1,0:T(8,128)(2,1)} %coeffs_ref.1) | copy-start | bytes 1572868
  1.0 1.0 %copy-start.1 = (bf16[1,128,1280]{2,1,0:T(8,128)(2,1)S(1)}, bf16[1,128,1280]{2,1,0:T(8,128)(2,1)}, u32[]{:S(2)}) copy-start(bf16[1,128,1280]{2,1,0:T(8,128)(2,1)} %panels_ref.1) | copy-start | bytes 983044
  2.0 0.9 %copy-start.2 = (bf16[1,128,512]{2,1,0:T(8,128)(2,1)S(1)}, bf16[1,128,512]{2,1,0:T(8,128)(2,1)}, u32[]{:S(2)}) copy-start(bf16[1,128,512]{2,1,0:T(8,128)(2,1)} %refl_ref.1) | copy-start | bytes 393220
  2.9 0.7 %copy-start.3 = (s32[1,256]{1,0:T(1,128)S(1)}, s32[1,256]{1,0:T(1,128)}, u32[]{:S(2)}) copy-start(s32[1,256]{1,0:T(1,128)} %cmap_ref.1) | copy-start | bytes 3076
  3.6 0.7 %copy-start.4 = (s32[1,1,4]{2,1,0:T(1,128)S(1)}, s32[1,1,4]{2,1,0:T(1,128)}, u32[]{:S(2)}) copy-start(s32[1,1,4]{2,1,0:T(1,128)} %mask_ref.1) | copy-start | bytes 52
  4.3 0.7 %copy-start.5 = (s32[1,4]{1,0:T(1,128)S(1)}, s32[1,4]{1,0:T(1,128)}, u32[]{:S(2)}) copy-start(s32[1,4]{1,0:T(1,128)} %starts_ref.1) | copy-start | bytes 52

commit v2 on v1

v2 whole, which is shorter than its diff:
```python
import functools

import jax
import jax.numpy as jnp
from jax import lax
from jax.experimental import pallas as pl
from jax.experimental.pallas import tpu as pltpu
from jax.sharding import PartitionSpec as P

F32 = jnp.float32
BF16 = jnp.bfloat16
LANES = 128


def dot(a, b):
    return jnp.dot(a, b, preferred_element_type=F32)


def dot_nt(a, b):
    return lax.dot_general(a, b, (((1,), (1,)), ((), ())), preferred_element_type=F32)


def kernel(
    n, fronts, bounds, width,
    mask_hbm, starts_hbm, panels_hbm, refl_hbm, coeffs_hbm, cmap_hbm, out_ref,
    mask, starts, panels, refl, coeffs, cmap,
    pt, pr, ea, place, ec, step, step_in, tails, tail_in, cout, cin, carry, sacc, rt, rr,
    in_sem, e_send, e_recv, s_send, s_recv, p_send, p_recv, r_send, r_recv,
    t_send, t_recv, c_send, d_send, c_recv, m_send, m_recv,
):
    me = lax.axis_index("row")
    front = lax.axis_index("front")
    span = panels.shape[1]
    cols = panels.shape[2]
    rows = n * span
    tail = 3 * rows // 4
    chips = n // 2
    chip = me // 2
    core = me % 2
    sibling = chip * 2 + (1 - core)
    mesh_id = pl.DeviceIdType.MESH

    def at_row(r):
        return {"front": front, "row": r}

    def at_front(f):
        return {"front": f, "row": me}

    def remote(src, dst, ss, rs, dev):
        return pltpu.make_async_remote_copy(
            src_ref=src, dst_ref=dst, send_sem=ss, recv_sem=rs,
            device_id=dev, device_id_type=mesh_id,
        )

    def blk(r):
        return pl.ds(pl.multiple_of(r * span, span), span)

    def strip(r, lo, hi):
        return pl.ds(pl.multiple_of(r * width + lo, 16), hi - lo)

    loads = [
        pltpu.make_async_copy(src, dst, in_sem.at[i])
        for i, (src, dst) in enumerate([
            (mask_hbm, mask), (starts_hbm, starts), (refl_hbm, refl),
            (panels_hbm, panels), (cmap_hbm, cmap), (coeffs_hbm, coeffs)])
    ]
    for load in loads:
        load.start()

    barrier = pltpu.get_barrier_semaphore()
    for k in range(1, n):
        pl.semaphore_signal(barrier, inc=1, device_id=at_row((me + k) % n),
                            device_id_type=mesh_id)
    greeted = n - 1
    for d in (-2, -1, 1, 2):
        there = jnp.logical_and(front + d >= 0, front + d < fronts)
        greeted = greeted + jnp.where(there, 1, 0)

        @pl.when(there)
        def _(d=d):
            pl.semaphore_signal(barrier, inc=1, device_id=at_front(front + d),
                                device_id_type=mesh_id)

    for load in loads[:3]:
        load.wait()
    row_ids = me * span + lax.broadcasted_iota(jnp.int32, (span, LANES), 0)
    for j in range(refl.shape[2] // LANES):
        keep = jnp.logical_and(row_ids >= starts[0, j], mask[0, 0, j] == 1)
        block = refl[0, :, j * LANES:(j + 1) * LANES]
        ea[blk(me), j * LANES:(j + 1) * LANES] = jnp.where(keep, block, jnp.zeros_like(block))

    pl.semaphore_wait(barrier, greeted)

    e_out = []
    for k in range(1, chips):
        c = remote(ea.at[blk(me)], ea.at[blk(me)], e_send.at[k], e_recv.at[k],
                   at_row(((chip + k) % chips) * 2 + core))
        c.start()
        e_out.append(c)
    c = remote(ea.at[blk(me)], ea.at[blk(me)], s_send.at[0], s_recv.at[0], at_row(sibling))
    c.start()
    e_out.append(c)

    loads[3].wait()
    for j in range(cols // LANES):
        pt[j * LANES:(j + 1) * LANES, :] = panels[0, :, j * LANES:(j + 1) * LANES].T
    if pt.shape[0] > cols:
        pt[cols:, :] = jnp.zeros((pt.shape[0] - cols, span), BF16)
    p_out = []
    for h, (lo, hi) in enumerate(bounds):
        for k in range(1, n):
            peer = (me + k) % n
            c = remote(pt.at[strip(peer, lo, hi)], pr.at[pl.ds(lo, hi - lo), blk(me)],
                       p_send.at[h, k], p_recv.at[h, k], at_row(peer))
            c.start()
            p_out.append(c)
    pr[:, blk(me)] = pt[strip(me, 0, width), :]

    loads[4].wait()
    ncar = cmap.shape[1]
    targets = jnp.broadcast_to(cmap[...], (LANES, ncar)).T
    lane = lax.broadcasted_iota(jnp.int32, (ncar, LANES), 1)
    for b in range(rows // LANES):
        place[:, b * LANES:(b + 1) * LANES] = jnp.where(
            targets == lane + b * LANES, 1.0, 0.0).astype(BF16)
    loads[5].wait()

    for k in range(1, chips):
        src = ((chip + chips - k) % chips) * 2 + core
        e_out[k - 1].wait_recv()
        c = remote(ea.at[blk(src)], ea.at[blk(src)], s_send.at[k], s_recv.at[k], at_row(sibling))
        c.start()
        e_out.append(c)
    for c in e_out[chips - 1:]:
        c.wait_recv()

    ec[...] = dot(place[...], ea[...]).astype(BF16)
    through = dot(ec[...], coeffs[0]).astype(BF16)
    step[...] = (place[:, tail:].astype(F32) - dot_nt(through, ea[tail:, :])).astype(BF16)

    even = front % 2 == 0
    has_next = front + 1 < fronts
    feeds = jnp.logical_and(even, has_next)
    feeds_map = jnp.logical_and(feeds, front > 0)
    odd_next = jnp.logical_and(front % 2 == 1, has_next)
    odd_after = jnp.logical_and(front % 2 == 1, front + 2 < fronts)
    odd_late = jnp.logical_and(front % 2 == 1, front > 1)
    even_late = jnp.logical_and(even, front > 0)

    m_copy = remote(step, step_in, m_send, m_recv, at_front(lax.rem(front + 1, fronts)))

    @pl.when(feeds_map)
    def _():
        m_copy.start()

    t_copies, c_copies, d_copies, r_out = [], [], [], []
    for h, (lo, hi) in enumerate(bounds):
        part = pl.ds(lo, hi - lo)
        t_copies.append(remote(tails.at[part], tail_in.at[part], t_send.at[h], t_recv.at[h],
                               at_front(lax.rem(front + 1, fronts))))
        c_copies.append(remote(cout.at[part], cin.at[part], c_send.at[h], c_recv.at[h],
                               at_front(lax.rem(front + 1, fronts))))
        d_copies.append(remote(cout.at[part], cin.at[part], d_send.at[h], c_recv.at[h],
                               at_front(lax.rem(front + 2, fronts))))

    for h, (lo, hi) in enumerate(bounds):
        for c in p_out[h * (n - 1):(h + 1) * (n - 1)]:
            c.wait_recv()
        total = dot(pr[lo:hi, :], ea[...])
        sacc[lo:hi, :] = total
        mixed = dot(total.astype(BF16), coeffs[0]).astype(BF16)
        tails[lo:hi, :] = (
            pr[lo:hi, tail:].astype(F32) - dot_nt(mixed, ea[tail:, :])).astype(BF16)

        @pl.when(feeds)
        def _(h=h):
            t_copies[h].start()

    for h, (lo, hi) in enumerate(bounds):
        @pl.when(front == 0)
        def _():
            carry[lo:hi, :] = jnp.zeros((hi - lo, ncar), BF16)

        @pl.when(front == 1)
        def _():
            t_copies[h].wait_recv()
            carry[lo:hi, :] = tail_in[lo:hi, :]

        @pl.when(even_late)
        def _():
            c_copies[h].wait_recv()
            carry[lo:hi, :] = cin[lo:hi, :]

        @pl.when(odd_late)
        def _():
            if h == 0:
                m_copy.wait_recv()
            t_copies[h].wait_recv()
            c_copies[h].wait_recv()
            carry[lo:hi, :] = (tail_in[lo:hi, :].astype(F32)
                               + dot(cin[lo:hi, :], step_in[...])).astype(BF16)

        @pl.when(odd_next)
        def _():
            cout[lo:hi, :] = (tails[lo:hi, :].astype(F32)
                              + dot(carry[lo:hi, :], step[...])).astype(BF16)

        @pl.when(odd_after)
        def _():
            d_copies[h].start()

        @pl.when(odd_next)
        def _():
            c_copies[h].start()

        carried = carry[lo:hi, :]
        wcoef = (sacc[lo:hi, :] + dot(carried, ec[...])).astype(BF16)
        mixed = dot(wcoef, coeffs[0]).astype(BF16)
        assembled = (pr[lo:hi, :].astype(F32) + dot(carried, place[...])).astype(BF16)
        rt[lo:hi, :] = (assembled.astype(F32) - dot_nt(mixed, ea[...])).astype(BF16)
        for k in range(1, n):
            peer = (me + k) % n
            c = remote(rt.at[pl.ds(lo, hi - lo), blk(peer)], rr.at[strip(me, lo, hi)],
                       r_send.at[h, k], r_recv.at[h, k], at_row(peer))
            c.start()
            r_out.append(c)
        rr[strip(me, lo, hi), :] = rt[lo:hi, blk(me)]

    for c in r_out:
        c.wait_recv()
    for j in range(cols // LANES):
        out_ref[0, :, j * LANES:(j + 1) * LANES] = rr[j * LANES:(j + 1) * LANES, :].T

    for c in e_out + p_out + r_out:
        c.wait_send()
    for flag, copies in ((feeds_map, [m_copy]), (feeds, t_copies),
                         (odd_after, d_copies), (odd_next, c_copies)):
        @pl.when(flag)
        def _(copies=copies):
            for c in copies:
                c.wait_send()


def local(n, fronts, panels, reflectors, block_coeffs, block_mask, block_starts, carry_map):
    _, span, cols = panels.shape
    k = reflectors.shape[2]
    rows = n * span
    ncar = carry_map.shape[1]
    width = -(-cols // (16 * n)) * 16
    half = width // 32 * 16
    bounds = ((0, half), (half, width))
    parts = len(bounds)
    dma = pltpu.SemaphoreType.DMA
    hbm = pl.BlockSpec(memory_space=pltpu.HBM)
    return pl.pallas_call(
        functools.partial(kernel, n, fronts, bounds, width),
        out_shape=jax.ShapeDtypeStruct(panels.shape, panels.dtype),
        in_specs=[hbm] * 6,
        out_specs=pl.BlockSpec(memory_space=pltpu.VMEM),
        scratch_shapes=[
            pltpu.SMEM(block_mask.shape, jnp.int32),
            pltpu.SMEM(block_starts.shape, jnp.int32),
            pltpu.VMEM(panels.shape, BF16),
            pltpu.VMEM(reflectors.shape, BF16),
            pltpu.VMEM(block_coeffs.shape, BF16),
            pltpu.VMEM(carry_map.shape, jnp.int32),
            pltpu.VMEM((n * width, span), BF16),
            pltpu.VMEM((width, rows), BF16),
            pltpu.VMEM((rows, k), BF16),
            pltpu.VMEM((ncar, rows), BF16),
            pltpu.VMEM((ncar, k), BF16),
            pltpu.VMEM((ncar, ncar), BF16),
            pltpu.VMEM((ncar, ncar), BF16),
            pltpu.VMEM((width, ncar), BF16),
            pltpu.VMEM((width, ncar), BF16),
            pltpu.VMEM((width, ncar), BF16),
            pltpu.VMEM((width, ncar), BF16),
            pltpu.VMEM((width, ncar), BF16),
            pltpu.VMEM((width, k), F32),
            pltpu.VMEM((width, rows), BF16),
            pltpu.VMEM((n * width, span), BF16),
            dma((6,)),
            dma((n // 2,)), dma((n // 2,)), dma((n // 2,)), dma((n // 2,)),
            dma((parts, n)), dma((parts, n)), dma((parts, n)), dma((parts, n)),
            dma((parts,)), dma((parts,)), dma((parts,)), dma((parts,)), dma((parts,)),
            dma, dma,
        ],
        compiler_params=pltpu.CompilerParams(
            collective_id=0, has_side_effects=True, vmem_limit_bytes=56 * 1024 * 1024),
    )(block_mask, block_starts, panels, reflectors, block_coeffs, carry_map)


def solution(mesh):
    in_specs = (
        P("front", "row", None),
        P("front", "row", None),
        P("front", None, None),
        P("front", "row", None),
        P("front", None),
        P("front", None),
    )
    body = functools.partial(local, mesh.shape["row"], mesh.shape["front"])
    return jax.shard_map(body, mesh=mesh, in_specs=in_specs,
                         out_specs=P("front", "row", None), check_vma=False)
```

time: 36.9 us -> 29.9 us (0.81)
  the two profiles are of different devices: /device:TPU:25 before, /device:TPU:17 now
where the time goes in v2:
time: 29.9 us; the launch traced here: 29.7 us
  Pallas kernels  28 us (94%)
  local copies, waits for them, and re-layouts  1.72 us (6%)
    pallas_call x1, Pallas kernels, local(): pl.pallas_call(functools.partial(kernel, n, fronts, bounds, width), out_s...  28 us
    unnamed x1, local copies, waits for them, and re-layouts  1.72 us

profile of v2, /device:TPU:17, one launch (start us, length us, event | category | flops | bytes accessed | tf_op | source)
XLA Modules:
  0.0 29.7 jit_solution(1565440991111480223)
XLA Ops:
  0.0 28.0 %shard_map.64 = bf16[1,128,1280]{2,1,0:T(8,128)(2,1)} custom-call(s32[1,1,4]{2,1,0:T(1,128)} %mask_hbm.1, s32[1,4]{1,0:T(1,128)} %starts_hbm.1, bf16[1,128,1280]{2,1,0:T(8,128)(2,1)} %panels_hbm.1, bf16[1,128,512]{2,1,0:T(8,128)(2,1)} %refl_hbm.1, bf16[1,512,512]{2,1,0:T(8,128)(2,1)} %coeffs_hbm.1, s32[1,256]{1,0:T(1,128)} %cmap_hbm.1), custom_call_target="tpu_custom_call" | custom-call | tf_op jit(solution)/shard_map/pallas_call | solution.py:255
  28.0 1.7 %copy.8 = bf16[1,128,1280]{2,1,0:T(8,128)(2,1)} copy(bf16[1,128,1280]{2,1,0:T(8,128)(2,1)} %shard_map.64) | data formatting | bytes 655360

commit v3 on v2

--- a/solution.py
+++ b/solution.py
@@ -24,7 +24,7 @@
     n, fronts, bounds, width,
     mask_hbm, starts_hbm, panels_hbm, refl_hbm, coeffs_hbm, cmap_hbm, out_ref,
     mask, starts, panels, refl, coeffs, cmap,
-    pt, pr, ea, place, ec, step, step_in, tails, tail_in, cout, cin, carry, sacc, rt, rr,
+    pt, pr, ea, place, step, step_in, tails, tail_in, cout, cin, carry, mix, rest, rt, rr,
     in_sem, e_send, e_recv, s_send, s_recv, p_send, p_recv, r_send, r_recv,
     t_send, t_recv, c_send, d_send, c_recv, m_send, m_recv,
 ):
@@ -134,10 +134,6 @@
     for c in e_out[chips - 1:]:
         c.wait_recv()
 
-    ec[...] = dot(place[...], ea[...]).astype(BF16)
-    through = dot(ec[...], coeffs[0]).astype(BF16)
-    step[...] = (place[:, tail:].astype(F32) - dot_nt(through, ea[tail:, :])).astype(BF16)
-
     even = front % 2 == 0
     has_next = front + 1 < fronts
     feeds = jnp.logical_and(even, has_next)
@@ -147,11 +143,8 @@
     odd_late = jnp.logical_and(front % 2 == 1, front > 1)
     even_late = jnp.logical_and(even, front > 0)
 
-    m_copy = remote(step, step_in, m_send, m_recv, at_front(lax.rem(front + 1, fronts)))
-
-    @pl.when(feeds_map)
-    def _():
-        m_copy.start()
+    m_copy = remote(step.at[:, pl.ds(tail, rows - tail)], step_in, m_send, m_recv,
+                    at_front(lax.rem(front + 1, fronts)))
 
     t_copies, c_copies, d_copies, r_out = [], [], [], []
     for h, (lo, hi) in enumerate(bounds):
@@ -166,21 +159,43 @@
     for h, (lo, hi) in enumerate(bounds):
         for c in p_out[h * (n - 1):(h + 1) * (n - 1)]:
             c.wait_recv()
-        total = dot(pr[lo:hi, :], ea[...])
-        sacc[lo:hi, :] = total
-        mixed = dot(total.astype(BF16), coeffs[0]).astype(BF16)
-        tails[lo:hi, :] = (
-            pr[lo:hi, tail:].astype(F32) - dot_nt(mixed, ea[tail:, :])).astype(BF16)
+        wcoef = dot(pr[lo:hi, :], ea[...]).astype(BF16)
+        mix[lo:hi, :] = dot(wcoef, coeffs[0]).astype(BF16)
+        own = pr[lo:hi, tail:].astype(F32) - dot_nt(mix[lo:hi, :], ea[tail:, :])
+        tails[lo:hi, :] = own.astype(BF16)
+        rest[lo:hi, tail:] = own
 
         @pl.when(feeds)
         def _(h=h):
             t_copies[h].start()
 
+    ec = dot(place[...], ea[...]).astype(BF16)
+    through = dot(ec, coeffs[0]).astype(BF16)
+
+    def map_columns(lo, hi):
+        step[:, lo:hi] = (place[:, lo:hi].astype(F32)
+                          - dot_nt(through, ea[lo:hi, :])).astype(BF16)
+
+    map_columns(tail, rows)
+
+    @pl.when(feeds_map)
+    def _():
+        m_copy.start()
+
+    def rest_rows(lo, hi):
+        rest[lo:hi, :tail] = pr[lo:hi, :tail].astype(F32) - dot_nt(mix[lo:hi, :], ea[:tail, :])
+
+    @pl.when(front == 0)
+    def _():
+        for lo, hi in bounds:
+            rest_rows(lo, hi)
+
+    @pl.when(front > 0)
+    def _():
+        map_columns(0, tail)
+        rest_rows(0, width)
+
     for h, (lo, hi) in enumerate(bounds):
-        @pl.when(front == 0)
-        def _():
-            carry[lo:hi, :] = jnp.zeros((hi - lo, ncar), BF16)
-
         @pl.when(front == 1)
         def _():
             t_copies[h].wait_recv()
@@ -203,7 +218,7 @@
         @pl.when(odd_next)
         def _():
             cout[lo:hi, :] = (tails[lo:hi, :].astype(F32)
-                              + dot(carry[lo:hi, :], step[...])).astype(BF16)
+                              + dot(carry[lo:hi, :], step[:, tail:])).astype(BF16)
 
         @pl.when(odd_after)
         def _():
@@ -213,11 +228,14 @@
         def _():
             c_copies[h].start()
 
-        carried = carry[lo:hi, :]
-        wcoef = (sacc[lo:hi, :] + dot(carried, ec[...])).astype(BF16)
-        mixed = dot(wcoef, coeffs[0]).astype(BF16)
-        assembled = (pr[lo:hi, :].astype(F32) + dot(carried, place[...])).astype(BF16)
-        rt[lo:hi, :] = (assembled.astype(F32) - dot_nt(mixed, ea[...])).astype(BF16)
+        @pl.when(front == 0)
+        def _():
+            rt[lo:hi, :] = rest[lo:hi, :].astype(BF16)
+
+        @pl.when(front > 0)
+        def _():
+            rt[lo:hi, :] = (rest[lo:hi, :] + dot(carry[lo:hi, :], step[...])).astype(BF16)
+
         for k in range(1, n):
             peer = (me + k) % n
             c = remote(rt.at[pl.ds(lo, hi - lo), blk(peer)], rr.at[strip(me, lo, hi)],
@@ -268,15 +286,15 @@
             pltpu.VMEM((width, rows), BF16),
             pltpu.VMEM((rows, k), BF16),
             pltpu.VMEM((ncar, rows), BF16),
-            pltpu.VMEM((ncar, k), BF16),
+            pltpu.VMEM((ncar, rows), BF16),
             pltpu.VMEM((ncar, ncar), BF16),
-            pltpu.VMEM((ncar, ncar), BF16),
-            pltpu.VMEM((width, ncar), BF16),
-            pltpu.VMEM((width, ncar), BF16),
-            pltpu.VMEM((width, ncar), BF16),
-            pltpu.VMEM((width, ncar), BF16),
-            pltpu.VMEM((width, ncar), BF16),
-            pltpu.VMEM((width, k), F32),
+            pltpu.VMEM((width, ncar), BF16),
+            pltpu.VMEM((width, ncar), BF16),
+            pltpu.VMEM((width, ncar), BF16),
+            pltpu.VMEM((width, ncar), BF16),
+            pltpu.VMEM((width, ncar), BF16),
+            pltpu.VMEM((width, k), BF16),
+            pltpu.VMEM((width, rows), F32),
             pltpu.VMEM((width, rows), BF16),
             pltpu.VMEM((n * width, span), BF16),
             dma((6,)),

time: 29.9 us -> 30.8 us (1.030)
  the two profiles are of different devices: /device:TPU:17 before, /device:TPU:25 now
where the time goes in v3:
time: 30.8 us; the launch traced here: 30.6 us
  Pallas kernels  28.9 us (94%)
  local copies, waits for them, and re-layouts  1.72 us (6%)
    pallas_call x1, Pallas kernels, local(): pl.pallas_call(functools.partial(kernel, n, fronts, bounds, width), out_s...  28.9 us
    unnamed x1, local copies, waits for them, and re-layouts  1.72 us

profile of v3, /device:TPU:25, one launch (start us, length us, event | category | flops | bytes accessed | tf_op | source)
XLA Modules:
  0.0 30.6 jit_solution(3453298290740018464)
XLA Ops:
  0.0 28.9 %shard_map.64 = bf16[1,128,1280]{2,1,0:T(8,128)(2,1)} custom-call(s32[1,1,4]{2,1,0:T(1,128)} %mask_hbm.1, s32[1,4]{1,0:T(1,128)} %starts_hbm.1, bf16[1,128,1280]{2,1,0:T(8,128)(2,1)} %panels_hbm.1, bf16[1,128,512]{2,1,0:T(8,128)(2,1)} %refl_hbm.1, bf16[1,512,512]{2,1,0:T(8,128)(2,1)} %coeffs_hbm.1, s32[1,256]{1,0:T(1,128)} %cmap_hbm.1), custom_call_target="tpu_custom_call" | custom-call | tf_op jit(solution)/shard_map/pallas_call | solution.py:273
  28.9 1.7 %copy.8 = bf16[1,128,1280]{2,1,0:T(8,128)(2,1)} copy(bf16[1,128,1280]{2,1,0:T(8,128)(2,1)} %shard_map.64) | data formatting | bytes 655360

commit v4 on v3

--- a/solution.py
+++ b/solution.py
@@ -190,7 +190,7 @@
         for lo, hi in bounds:
             rest_rows(lo, hi)
 
-    @pl.when(front > 0)
+    @pl.when(front > 1)
     def _():
         map_columns(0, tail)
         rest_rows(0, width)
@@ -228,6 +228,12 @@
         def _():
             c_copies[h].start()
 
+    @pl.when(front == 1)
+    def _():
+        map_columns(0, tail)
+        rest_rows(0, width)
+
+    for h, (lo, hi) in enumerate(bounds):
         @pl.when(front == 0)
         def _():
             rt[lo:hi, :] = rest[lo:hi, :].astype(BF16)

time: 30.8 us -> 30.9 us (level)
  no operation moved by 1% of the time
where the time goes in v4:
time: 30.9 us; the launch traced here: 30.8 us
  Pallas kernels  29.1 us (94%)
  local copies, waits for them, and re-layouts  1.72 us (6%)
    pallas_call x1, Pallas kernels, local(): pl.pallas_call(functools.partial(kernel, n, fronts, bounds, width), out_s...  29.1 us
    unnamed x1, local copies, waits for them, and re-layouts  1.72 us

profile of v4, /device:TPU:25, one launch (start us, length us, event | category | flops | bytes accessed | tf_op | source)
XLA Modules:
  0.0 30.8 jit_solution(14971851270357442475)
XLA Ops:
  0.0 29.1 %shard_map.64 = bf16[1,128,1280]{2,1,0:T(8,128)(2,1)} custom-call(s32[1,1,4]{2,1,0:T(1,128)} %mask_hbm.1, s32[1,4]{1,0:T(1,128)} %starts_hbm.1, bf16[1,128,1280]{2,1,0:T(8,128)(2,1)} %panels_hbm.1, bf16[1,128,512]{2,1,0:T(8,128)(2,1)} %refl_hbm.1, bf16[1,512,512]{2,1,0:T(8,128)(2,1)} %coeffs_hbm.1, s32[1,256]{1,0:T(1,128)} %cmap_hbm.1), custom_call_target="tpu_custom_call" | custom-call | tf_op jit(solution)/shard_map/pallas_call | solution.py:279
  29.1 1.7 %copy.8 = bf16[1,128,1280]{2,1,0:T(8,128)(2,1)} copy(bf16[1,128,1280]{2,1,0:T(8,128)(2,1)} %shard_map.64) | data formatting | bytes 655360
